TPU v7x, 512 devices: a whole 4x4x16 slice. The times are simulated.
512 devices in a mesh: section: 2 (over x_hi), gy: 16 (over y, x_lo, core), gx: 16 (over z).
Axes of the slice: x: 4 (x_hi: 2, x_lo: 2; x = x_hi * 2 + x_lo), y: 4, z: 16, core: 2. Of those that a mesh axis runs over, the one named last changes fastest.
Arguments:
- images: bfloat16 [2, 512, 1024, 128], P('section', 'gy', 'gx'), may hold values from -6 to 6
- first_kernel: bfloat16 [3, 3, 128, 128], replicated, may hold values from -0.1875 to 0.1875
- projection: bfloat16 [128, 256], replicated, may hold values from -0.5 to 0.5
- second_kernel: bfloat16 [3, 3, 256, 256], replicated, may hold values from -0.125 to 0.125
- cotangent: bfloat16 [2, 256, 512, 256], P('section', 'gy', 'gx'), may hold values from -0.15625 to 0.15625
Outputs:
- features: bfloat16 [2, 256, 512, 256], P('section', 'gy', 'gx')
- grad_first: float32 [3, 3, 128, 128], replicated
- grad_projection: float32 [128, 256], replicated
- grad_second: float32 [3, 3, 256, 256], replicated
All inputs are finite; a program needn't handle non-finite values.
Results may differ from a plain program's by a relative error of at most 0.014.
Values may be sent and summed in bfloat16 or wider, within the bound.
A program may use at most 64 MiB of HBM per device.

v0:
```python
import jax
import jax.numpy as jnp
from jax import lax
from jax.sharding import PartitionSpec as P


def padded_2(array, sides, width):
    for axis, dim in sides:
        size, length = (lax.axis_size(axis), array.shape[dim])
        up = [(i, (i + 1) % size) for i in range(size - 1)]
        down = [(j, i) for i, j in up]
        last = lax.slice_in_dim(array, length - width, length, axis=dim)
        initial = lax.slice_in_dim(array, 0, width, axis=dim)
        before = lax.ppermute(last, axis, up)
        after = lax.ppermute(initial, axis, down)
        array = jnp.concatenate([before, array, after], axis=dim)
    return array


def from_partner(block, axis, bit):
    count = lax.axis_size(axis)
    route = []
    for low in range(count):
        high = low | 1 << bit
        if high != low and high < count:
            route += [(low, high), (high, low)]
    return lax.ppermute(block, axis, route)


def silu_slope(values):
    sigma = jax.nn.sigmoid(values)
    return sigma * (1.0 + values * (1.0 - sigma))


def conv_forward(padded, kernel, row_count, col_count):
    total = jnp.zeros((row_count * col_count, kernel.shape[3]), jnp.float32)
    for row_tap in range(3):
        for col_tap in range(3):
            piece = padded[row_tap : row_tap + row_count, col_tap : col_tap + col_count].reshape(
                row_count * col_count, padded.shape[2]
            )
            total = total + jnp.dot(
                piece, kernel[row_tap, col_tap], preferred_element_type=jnp.float32
            )
    return total


def conv_slopes(padded, slope, row_count, col_count):
    pieces = []
    for row_tap in range(3):
        for col_tap in range(3):
            piece = padded[row_tap : row_tap + row_count, col_tap : col_tap + col_count].reshape(
                row_count * col_count, padded.shape[2]
            )
            pieces.append(jnp.einsum("pc,pd->cd", piece, slope, preferred_element_type=jnp.float32))
    return jnp.stack(pieces).reshape(3, 3, padded.shape[2], slope.shape[1])


def conv_back(padded, kernel, row_count, col_count):
    total = jnp.zeros((row_count * col_count, kernel.shape[2]), jnp.float32)
    for row_tap in range(3):
        for col_tap in range(3):
            piece = padded[
                2 - row_tap : 2 - row_tap + row_count, 2 - col_tap : 2 - col_tap + col_count
            ].reshape(row_count * col_count, padded.shape[2])
            total = total + jnp.einsum(
                "pd,cd->pc", piece, kernel[row_tap, col_tap], preferred_element_type=jnp.float32
            )
    return total


def first_forward(tile, first_kernel):
    row_count, col_count, channels = tile.shape
    padded = padded_2(tile, (("gy", 0), ("gx", 1)), 1)
    before = conv_forward(padded, first_kernel, row_count, col_count)
    hidden = jax.nn.silu(before).astype(jnp.bfloat16).reshape(row_count, col_count, channels)
    pooled = (
        hidden.astype(jnp.float32)
        .reshape(row_count // 2, 2, col_count // 2, 2, channels)
        .sum(axis=(1, 3))
        * 0.25
    ).astype(jnp.bfloat16)
    return (padded, before, pooled)


def project(pooled, projection):
    half_rows, half_cols, channels = pooled.shape
    flat = jnp.dot(
        pooled.reshape(half_rows * half_cols, channels),
        projection,
        preferred_element_type=jnp.float32,
    )
    return flat.astype(jnp.bfloat16).reshape(half_rows, half_cols, projection.shape[1])


def second_pass(middle, second_kernel, upstream):
    half_rows, half_cols, wide = middle.shape
    padded = padded_2(middle, (("gy", 0), ("gx", 1)), 1)
    before = conv_forward(padded, second_kernel, half_rows, half_cols)
    output = jax.nn.silu(before).astype(jnp.bfloat16).reshape(half_rows, half_cols, wide)
    flat_up = upstream.reshape(half_rows * half_cols, wide).astype(jnp.float32)
    slope = (flat_up * silu_slope(before)).astype(jnp.bfloat16)
    kernel_grad = conv_slopes(padded, slope, half_rows, half_cols)
    slope_padded = padded_2(slope.reshape(half_rows, half_cols, wide), (("gy", 0), ("gx", 1)), 1)
    back = conv_back(slope_padded, second_kernel, half_rows, half_cols).astype(jnp.bfloat16)
    return (output, kernel_grad, back.reshape(half_rows, half_cols, wide))


def projection_back(pooled, back, projection):
    half_rows, half_cols, channels = pooled.shape
    flat_pool = pooled.reshape(half_rows * half_cols, channels)
    flat_back = back.reshape(half_rows * half_cols, back.shape[2])
    grad = jnp.einsum("pc,pd->cd", flat_pool, flat_back, preferred_element_type=jnp.float32)
    pooled_slope = jnp.einsum(
        "pd,cd->pc", flat_back, projection, preferred_element_type=jnp.float32
    )
    return (grad, pooled_slope.astype(jnp.bfloat16).reshape(half_rows, half_cols, channels))


def first_back(padded, before, pooled_slope):
    half_rows, half_cols, channels = pooled_slope.shape
    spread = jnp.broadcast_to(
        (pooled_slope.astype(jnp.float32) * 0.25)[:, None, :, None, :],
        (half_rows, 2, half_cols, 2, channels),
    )
    spread = spread.reshape(4 * half_rows * half_cols, channels)
    slope = (spread * silu_slope(before)).astype(jnp.bfloat16)
    return conv_slopes(padded, slope, 2 * half_rows, 2 * half_cols)


def per_device(images, first_kernel, projection, second_kernel, cotangent):
    padded, before, pooled = first_forward(images[0], first_kernel)
    middle = from_partner(project(pooled, projection), "section", 0)
    output, grad_second, back_far = second_pass(middle, second_kernel, cotangent[0])
    back = from_partner(back_far, "section", 0)
    grad_projection, pooled_slope = projection_back(pooled, back, projection)
    grad_first = first_back(padded, before, pooled_slope)
    grad_first, grad_projection, grad_second = lax.psum(
        (grad_first, grad_projection, grad_second), ("section", "gy", "gx")
    )
    return (output[None], grad_first, grad_projection, grad_second)


def solution(mesh):
    placed = (P("section", "gy", "gx", None), P(), P(), P(), P("section", "gy", "gx", None))
    return jax.shard_map(
        per_device,
        mesh=mesh,
        in_specs=placed,
        out_specs=(P("section", "gy", "gx", None), P(), P(), P()),
        check_vma=False,
    )
```

profile of v0, /device:TPU:2, one launch (start us, length us, event | category | flops | bytes accessed | tf_op | source)
XLA Modules:
  0.0 605.1 jit_solution(15916452577856336045)
XLA Ops:
  7.2 0.8 slice_bitcast_fusion.3
  8.0 1.9 collective-permute-start
  10.0 3.6 collective-permute-start.1
  13.6 1.4 collective-permute-done.1
  15.0 0.9 pad_maximum_fusion.15
  15.9 3.8 collective-permute-start.2
  19.8 1.4 collective-permute-start.3
  21.2 1.3 pad_maximum_fusion.1
  22.8 2.7 collective-permute-done.3
  25.6 0.3 maximum_maximum_fusion
  25.9 0.6 fusion.93
  26.5 0.3 fusion.73
  28.5 0.5 multiply_convert_fusion.1
  29.0 0.9 convert_reduce_fusion
  30.1 4.1 collective-permute-start.4
  34.3 8.2 %collective-permute-done.4 = bf16[16,32,256]{2,1,0:T(8,128)(2,1)S(1)} collective-permute-done((bf16[16,32,256]{2,1,0:T(8,128)(2,1)S(1)}, bf16[16,32,256]{2,1,0:T(8,128)(2,1)S(1)}, u32[]{:S(2)}, u32[]{:S(2)}) %collective-permute-start.4) | collective-permute-done | bytes 262176 | tf_op jit(solution)/shard_map/ppermute | solution.py:27
  42.5 2.1 collective-permute-start.5
  44.6 3.5 collective-permute-start.6
  48.1 1.4 collective-permute-done.6
  49.6 3.8 collective-permute-start.7
  53.5 1.3 collective-permute-start.8
  55.3 4.9 collective-permute-done.8
  60.1 0.4 pad_maximum_fusion.8
  61.9 0.7 copy-done.7
  62.6 1.1 fusion.26
  64.1 3.1 collective-permute-start.9
  67.2 2.5 collective-permute-start.10
  71.4 1.3 collective-permute-start.11
  72.7 6.0 collective-permute-start.12
  79.0 1.1 collective-permute-done.12
  82.7 4.0 collective-permute-start.13
  87.2 7.4 %collective-permute-done.13 = bf16[16,32,256]{2,1,0:T(8,128)(2,1)S(1)} collective-permute-done((bf16[16,32,256]{2,1,0:T(8,128)(2,1)S(1)}, bf16[16,32,256]{2,1,0:T(8,128)(2,1)S(1)}, u32[]{:S(2)}, u32[]{:S(2)}) %collective-permute-start.13) | collective-permute-done | bytes 262176 | tf_op jit(solution)/shard_map/ppermute | solution.py:27
  94.9 0.5 broadcast_in_dim.2
  95.4 0.4 multiply_convert_fusion
  95.8 0.3 fusion.25
  96.1 0.4 fusion.24
  96.5 0.4 fusion.23
  96.9 0.4 fusion.22
  97.2 0.4 fusion.21
  97.6 0.4 fusion.20
  97.9 0.4 fusion.19
  98.3 0.4 fusion.18
  98.7 0.4 fusion.17
  99.0 0.9 convolution_bitcast_fusion.9
  99.9 492.5 %all-reduce.3.cloned.1.call-done = (f32[3,3,128,128]{3,2,1,0:T(8,128)}, f32[128,256]{1,0:T(8,128)}, f32[3,3,256,256]{3,2,1,0:T(8,128)}) async-done(((f32[3,3,128,128]{3,2,1,0:T(8,128)}, f32[128,256]{1,0:T(8,128)}, f32[3,3,256,256]{3,2,1,0:T(8,128)}), (f32[3,3,128,128]{3,2,1,0:T(8,128)}, f32[128,256]{1,0:T(8,128)}, f32[3,3,256,256]{3,2,1,0:T(8,128)})) %all-reduce.3.cloned.1.call-update) | async-done | bytes 3080208 | tf_op jit(solution)/shard_map/psum | solution.py:138
  592.4 2.0 copy.32
  594.4 0.7 copy.33
  595.0 3.2 copy.34
  (71 shorter events, 9.7 us)
Async XLA Ops:
  7.2 22.7 %copy-start = (bf16[128,256]{1,0:T(8,128)(2,1)S(1)}, bf16[128,256]{1,0:T(8,128)(2,1)}, u32[]{:S(2)}) copy-start(bf16[128,256]{1,0:T(8,128)(2,1)} %param.7) | copy-start | bytes 196612
  7.2 15.3 %copy-start.5 = (bf16[3,3,128,128]{3,2,1,0:T(8,128)(2,1)S(1)}, bf16[3,3,128,128]{3,2,1,0:T(8,128)(2,1)}, u32[]{:S(2)}) copy-start(bf16[3,3,128,128]{3,2,1,0:T(8,128)(2,1)} %param.6) | copy-start | bytes 884740
  7.2 585.2 %all-reduce.3.cloned.1.call-start = ((), (), s32[]{:S(2)}) async-start(), calls=%async_computation | async-start | bytes 6160384 | tf_op jit(solution)/shard_map/psum | solution.py:138
  8.0 5.6 collective-permute-start
  10.0 5.1 collective-permute-start.1
  15.9 6.9 %collective-permute-start.2 = (bf16[34,1,128]{2,1,0:T(2,128)(2,1)S(1)}, bf16[34,1,128]{2,1,0:T(2,128)(2,1)S(1)}, u32[]{:S(2)}, u32[]{:S(2)}) collective-permute-start(bf16[34,1,128]{2,1,0:T(2,128)(2,1)S(1)} %get-tuple-element.15), channel_id=1, source_target_pairs={{0,1},{1,2},{2,3},{3,4},{4,5},{5,6},{6,7},{7,8},{8,9},{9,10},{10,1... | collective-permute-start | bytes 26120 | tf_op jit(solution)/shard_map/ppermute | solution.py:14
  19.8 5.8 copy-start.1
  19.8 5.8 collective-permute-start.3
  29.9 24.9 %copy-start.2 = (bf16[3,3,256,256]{3,2,1,0:T(8,128)(2,1)S(1)}, bf16[3,3,256,256]{3,2,1,0:T(8,128)(2,1)}, u32[]{:S(2)}) copy-start(bf16[3,3,256,256]{3,2,1,0:T(8,128)(2,1)} %param.8) | copy-start | bytes 3538948
  30.1 12.4 %collective-permute-start.4 = (bf16[16,32,256]{2,1,0:T(8,128)(2,1)S(1)}, bf16[16,32,256]{2,1,0:T(8,128)(2,1)S(1)}, u32[]{:S(2)}, u32[]{:S(2)}) collective-permute-start(bf16[16,32,256]{2,1,0:T(8,128)(2,1)S(1)} %bitcast.328), channel_id=1, source_target_pairs={{0,256},{256,0},{1,257},{257,1},{2,258},{258,2},{3,259},{259,3},{4... | collective-permute-start | bytes 786440 | tf_op jit(solution)/shard_map/ppermute | solution.py:27
  42.5 5.6 collective-permute-start.5
  44.6 4.9 collective-permute-start.6
  49.6 5.6 collective-permute-start.7
  53.5 6.7 %collective-permute-start.8 = (bf16[18,1,256]{2,1,0:T(2,128)(2,1)S(1)}, bf16[18,1,256]{2,1,0:T(2,128)(2,1)S(1)}, u32[]{:S(2)}, u32[]{:S(2)}) collective-permute-start(bf16[18,1,256]{2,1,0:T(2,128)(2,1)S(1)} %get-tuple-element.43), channel_id=1, source_target_pairs={{1,0},{2,1},{3,2},{4,3},{5,4},{6,5},{7,6},{8,7},{9,8},{10,9},{11,1... | collective-permute-start | bytes 27656 | tf_op jit(solution)/shard_map/ppermute | solution.py:15
  61.7 1.0 copy-start.7
  64.1 7.3 %collective-permute-start.9 = (bf16[1,32,256]{2,1,0:T(8,128)(2,1)S(1)}, bf16[1,32,256]{2,1,0:T(8,128)(2,1)S(1)}, u32[]{:S(2)}, u32[]{:S(2)}) collective-permute-start(bf16[1,32,256]{2,1,0:T(8,128)(2,1)S(1)} %get-tuple-element.46), channel_id=1, source_target_pairs={{0,16},{16,32},{32,48},{48,64},{64,80},{80,96},{96,112},{112,128},... | collective-permute-start | bytes 49160 | tf_op jit(solution)/shard_map/ppermute | solution.py:14
  67.2 4.2 collective-permute-start.10
  71.4 7.6 %collective-permute-start.11 = (bf16[18,1,256]{2,1,0:T(2,128)(2,1)S(1)}, bf16[18,1,256]{2,1,0:T(2,128)(2,1)S(1)}, u32[]{:S(2)}, u32[]{:S(2)}) collective-permute-start(bf16[18,1,256]{2,1,0:T(2,128)(2,1)S(1)} %get-tuple-element.37), channel_id=1, source_target_pairs={{1,0},{2,1},{3,2},{4,3},{5,4},{6,5},{7,6},{8,7},{9,8},{10,9},{11,1... | collective-permute-start | bytes 27656 | tf_op jit(solution)/shard_map/ppermute | solution.py:15
  72.7 7.4 %collective-permute-start.12 = (bf16[18,1,256]{2,1,0:T(2,128)(2,1)S(1)}, bf16[18,1,256]{2,1,0:T(2,128)(2,1)S(1)}, u32[]{:S(2)}, u32[]{:S(2)}) collective-permute-start(bf16[18,1,256]{2,1,0:T(2,128)(2,1)S(1)} %get-tuple-element.38), channel_id=1, source_target_pairs={{0,1},{1,2},{2,3},{3,4},{4,5},{5,6},{6,7},{7,8},{8,9},{9,10},{10,1... | collective-permute-start | bytes 27656 | tf_op jit(solution)/shard_map/ppermute | solution.py:14
  82.7 12.0 %collective-permute-start.13 = (bf16[16,32,256]{2,1,0:T(8,128)(2,1)S(1)}, bf16[16,32,256]{2,1,0:T(8,128)(2,1)S(1)}, u32[]{:S(2)}, u32[]{:S(2)}) collective-permute-start(bf16[16,32,256]{2,1,0:T(8,128)(2,1)S(1)} %bitcast.329), channel_id=1, source_target_pairs={{0,256},{256,0},{1,257},{257,1},{2,258},{258,2},{3,259},{259,3},{4... | collective-permute-start | bytes 786440 | tf_op jit(solution)/shard_map/ppermute | solution.py:27
  87.2 8.6 %copy-start.3 = (f32[9,256,256]{2,1,0:T(8,128)}, f32[9,256,256]{2,1,0:T(8,128)S(1)}, u32[]{:S(2)}) copy-start(f32[9,256,256]{2,1,0:T(8,128)S(1)} %fusion.6) | copy-start | bytes 7077892
  99.0 0.9 copy-start.4
  592.4 2.0 copy-start.6
Sparse Core Ops, SparseCore 0:
  100.1 492.3 all-reduce.2
where the time goes:
time: 606 us; the launch traced here: 605 us
  waiting for transfers between devices  520 us (86%)
  starting transfers between devices  42.4 us (7%)
  matrix products  14.9 us (2%)
  between operations  14.7 us (2%)
  local copies, waits for them, and re-layouts  8.72 us (1%)
    psum x1, waiting for transfers between devices, per_device(): lax.psum((grad_first, grad_projection, grad_second), ('section', 'gy', 'g...  492 us
    ppermute x6, starting transfers between devices, padded_2(): before = lax.ppermute(last, axis, up)  20.7 us
    ppermute x2, waiting for transfers between devices, from_partner(): return lax.ppermute(block, axis, route)  15.7 us
    ppermute x6, starting transfers between devices, padded_2(): after = lax.ppermute(initial, axis, down)  13.6 us
  transfers between devices with their start and end apart: 15, of which 8 were waited for; matrix products, arithmetic and copies ran while one was open for 1% of the time, Pallas kernels for 0%

commit v1 on v0

--- a/solution.py
+++ b/solution.py
@@ -136,7 +136,7 @@
     grad_projection, pooled_slope = projection_back(pooled, back, projection)
     grad_first = first_back(padded, before, pooled_slope)
     grad_first, grad_projection, grad_second = lax.psum(
-        (grad_first, grad_projection, grad_second), ("section", "gy", "gx")
+        lax.psum((grad_first, grad_projection, grad_second), ("gy", "gx")), "section"
     )
     return (output[None], grad_first, grad_projection, grad_second)
 

time: 606 us -> 2310 us (3.81)
  the two profiles are of different devices: /device:TPU:2 before, /device:TPU:1 now
where the time goes in v1:
time: 2310 us
  waiting for transfers between devices  2220 us (96%)
  starting transfers between devices  45.8 us (2%)
    psum x1, waiting for transfers between devices, per_device(): lax.psum((grad_first, grad_projection, grad_second), ('gy', 'gx'))  2090 us
    psum x1, waiting for transfers between devices, per_device(): lax.psum(lax.psum((grad_first, grad_projection, grad_second), ('gy', 'gx'...  108 us
  transfers between devices with their start and end apart: 16, of which 10 were waited for; matrix products, arithmetic and copies ran while one was open for 0% of the time, Pallas kernels for 0%

profile of v1, /device:TPU:1, one launch (start us, length us, event | category | flops | bytes accessed | tf_op | source)
XLA Modules:
  0.0 2305.6 jit_solution(9248893497096286253)
XLA Ops:
  7.2 0.8 slice_bitcast_fusion.3
  8.0 4.5 collective-permute-start
  12.5 5.6 collective-permute-start.1
  18.1 0.8 collective-permute-done.1
  18.9 0.9 pad_maximum_fusion.15
  19.8 2.2 collective-permute-start.2
  22.1 1.4 collective-permute-start.3
  23.5 1.3 pad_maximum_fusion.1
  25.1 1.8 collective-permute-done.3
  27.2 0.6 fusion.93
  29.8 0.5 multiply_convert_fusion.1
  30.3 0.9 convert_reduce_fusion
  31.5 4.5 collective-permute-start.4
  36.0 6.5 collective-permute-done.4
  42.5 4.5 collective-permute-start.5
  47.0 1.9 collective-permute-start.6
  49.0 3.1 collective-permute-done.6
  52.2 3.6 collective-permute-start.7
  55.8 1.3 collective-permute-start.8
  57.6 4.0 collective-permute-done.8
  61.6 0.4 pad_maximum_fusion.8
  63.4 0.7 copy-done.7
  64.1 1.1 fusion.26
  65.5 3.1 collective-permute-start.9
  68.6 1.9 collective-permute-start.10
  72.2 1.4 collective-permute-done.10
  73.7 1.3 collective-permute-start.11
  75.0 5.7 collective-permute-start.12
  81.0 0.5 collective-permute-done.12
  84.1 4.3 collective-permute-start.13
  89.0 5.9 collective-permute-done.13
  95.2 0.5 broadcast_in_dim.2
  95.6 0.4 multiply_convert_fusion
  96.1 0.3 fusion.25
  96.4 0.4 fusion.24
  96.8 0.4 fusion.23
  97.1 0.4 fusion.22
  97.5 0.3 fusion.21
  97.8 0.4 fusion.20
  98.2 0.4 fusion.19
  98.6 0.4 fusion.18
  98.9 0.4 fusion.17
  99.3 0.9 convolution_bitcast_fusion.9
  100.3 2085.0 %all-reduce.5.cloned.1.call-done = (f32[3,3,128,128]{3,2,1,0:T(8,128)}, f32[128,256]{1,0:T(8,128)}, f32[3,3,256,256]{3,2,1,0:T(8,128)}) async-done(((f32[3,3,128,128]{3,2,1,0:T(8,128)}, f32[128,256]{1,0:T(8,128)}, f32[3,3,256,256]{3,2,1,0:T(8,128)}), (f32[3,3,128,128]{3,2,1,0:T(8,128)}, f32[128,256]{1,0:T(8,128)}, f32[3,3,256,256]{3,2,1,0:T(8,128)})) %all-reduce.5.cloned.1.call-update) | async-done | bytes 3080208 | tf_op jit(solution)/shard_map/psum | solution.py:139
  2185.3 107.7 %all-reduce.7.cloned.1.call-done = (f32[3,3,128,128]{3,2,1,0:T(8,128)}, f32[128,256]{1,0:T(8,128)}, f32[3,3,256,256]{3,2,1,0:T(8,128)}) async-done(((f32[3,3,128,128]{3,2,1,0:T(8,128)}, f32[128,256]{1,0:T(8,128)}, f32[3,3,256,256]{3,2,1,0:T(8,128)}), (f32[3,3,128,128]{3,2,1,0:T(8,128)}, f32[128,256]{1,0:T(8,128)}, f32[3,3,256,256]{3,2,1,0:T(8,128)})) %all-reduce.7.cloned.1.call-update) | async-done | bytes 3080208 | tf_op jit(solution)/shard_map/psum | solution.py:138
  2293.0 2.0 copy.35
  2294.9 0.7 copy.36
  2295.6 3.2 copy.37
  (74 shorter events, 10.4 us)
Async XLA Ops:
  7.2 24.1 %copy-start = (bf16[128,256]{1,0:T(8,128)(2,1)S(1)}, bf16[128,256]{1,0:T(8,128)(2,1)}, u32[]{:S(2)}) copy-start(bf16[128,256]{1,0:T(8,128)(2,1)} %param.7) | copy-start | bytes 196612
  7.2 17.6 copy-start.5
  7.2 2178.1 %all-reduce.5.cloned.1.call-start = ((), (), s32[]{:S(2)}) async-start(), calls=%async_computation | async-start | bytes 6160384 | tf_op jit(solution)/shard_map/psum | solution.py:139
  8.0 10.1 collective-permute-start
  12.5 6.4 collective-permute-start.1
  19.8 5.3 collective-permute-start.2
  22.1 4.8 copy-start.1
  22.1 4.8 collective-permute-start.3
  31.2 25.9 %copy-start.2 = (bf16[3,3,256,256]{3,2,1,0:T(8,128)(2,1)S(1)}, bf16[3,3,256,256]{3,2,1,0:T(8,128)(2,1)}, u32[]{:S(2)}) copy-start(bf16[3,3,256,256]{3,2,1,0:T(8,128)(2,1)} %param.8) | copy-start | bytes 3538948
  31.5 11.0 collective-permute-start.4
  42.5 6.5 collective-permute-start.5
  47.0 5.1 collective-permute-start.6
  52.2 5.3 collective-permute-start.7
  55.8 5.8 collective-permute-start.8
  63.1 1.0 copy-start.7
  65.5 6.7 collective-permute-start.9
  68.6 5.1 collective-permute-start.10
  73.7 7.3 collective-permute-start.11
  75.0 6.6 collective-permute-start.12
  84.1 10.8 collective-permute-start.13
  89.0 7.1 copy-start.3
  99.3 0.9 copy-start.4
  100.2 2192.7 %all-reduce.7.cloned.1.call-start = ((), (), s32[]{:S(2)}) async-start(), calls=%async_computation.1 | async-start | bytes 6160384 | tf_op jit(solution)/shard_map/psum | solution.py:138
  2293.0 2.0 copy-start.6
Sparse Core Ops, SparseCore 0:
  100.3 2084.8 all-reduce.4
  2188.6 104.2 all-reduce.6
